TPU v7x, 128 devices: a whole 4x4x4 slice. The times are simulated.
128 devices in a mesh: pb: 16 (over z_hi, y, core), ka: 8 (over z_lo, x).
Axes of the slice: x: 4, y: 4, z: 4 (z_hi: 2, z_lo: 2; z = z_hi * 2 + z_lo), core: 2. Of those that a mesh axis runs over, the one named last changes fastest.
Arguments:
- queries: bfloat16 [16384, 4096], P('pb'), may hold values from -6 to 6
- key_rows: bfloat16 [16384, 512], P(('pb', 'ka')), may hold values from -6 to 6
- values: bfloat16 [16384, 512], P(('pb', 'ka')), may hold values from -6 to 6
- attn_out: bfloat16 [16384, 4096], P(('pb', 'ka')), may hold values from -6 to 6
- grad_out: bfloat16 [16384, 4096], P('pb'), may hold values from -6 to 6
- log_sums: float32 [32, 16384], P(None, ('pb', 'ka')), may hold values from 3 to 7
- key_gain: float32 [512], replicated, may hold values from 0.25 to 1.75
- value_gain: float32 [512], replicated, may hold values from 0.25 to 1.75
- doc_ids: int32 [128], replicated, may hold values from 0 to 15, never falling along the last dimension, each value on 1 to 64 neighbouring positions
- tile_mask: int32 [128, 128], replicated, may hold values 0 or 1
- block_order: int32 [128], replicated, may hold values from 0 to 127, each once
Outputs:
- grad_queries: bfloat16 [16384, 4096], P(('pb', 'ka'))
- grad_keys: bfloat16 [16384, 512], P(('pb', 'ka'))
- grad_values: bfloat16 [16384, 512], P(('pb', 'ka'))
- grad_key_gain: float32 [512], replicated
- grad_value_gain: float32 [512], replicated
Inputs may be any that keep to these rules, and one draw needn't show every extreme that they name: `doc_ids`: documents are numbered in sequence order; each spans 1 to 64 tiles, one exactly that many. `block_order`: each sequence tile once.
All inputs are finite; a program needn't handle non-finite values.
Results may differ from a plain program's by a relative error of at most 0.015.
Values may be sent and summed in bfloat16 or wider, within the bound.
A program may use at most 192 MiB of HBM per device.

v0:
```python
import functools
import math

import jax
import jax.numpy as jnp
from jax import lax
from jax.experimental import pallas as pl
from jax.experimental.pallas import tpu as pltpu
from jax.sharding import PartitionSpec as P


D = 128
T = 128
RING = 4
KA = 8
HEADS = 4
WIDTH = HEADS * D
QUERY_TILES = 16
KEY_TILES = 64
Z_FIRST = 3
PARTS = 2
LOG2E = math.log2(math.e)
MESH = pl.DeviceIdType.MESH
F32 = jnp.float32
BF16 = jnp.bfloat16
NT = (((1,), (1,)), ((), ()))
TN = (((0,), (0,)), ((), ()))


def wrap(at):
    return lax.rem(at + RING, RING)


def place():
    pb, ka = lax.axis_index("pb"), lax.axis_index("ka")
    z = lax.div(pb, 8) * 2 + lax.div(ka, 4)
    return z, lax.rem(lax.div(pb, 2), 4), lax.rem(ka, 4), lax.rem(pb, 2)


def ident(z, y, x, c):
    return (lax.div(z, 2) * 8 + y * 2 + c, lax.rem(z, 2) * 4 + x)


def group_peers(z, y, x, c):
    ka = lax.rem(z, 2) * 4 + x
    peers = []
    for flip in range(2):
        for step in range(KA):
            if flip or step:
                to = lax.rem(ka + step, KA)
                core = 1 - c if flip else c
                peers.append((flip, step, ident(lax.div(z, 2) * 2 + lax.div(to, 4), y, lax.rem(to, 4), core)))
    return peers


def greet(devices):
    barrier = pltpu.get_barrier_semaphore()
    for device in devices:
        pl.semaphore_signal(barrier, inc=1, device_id=device, device_id_type=MESH)
    pl.semaphore_wait(barrier, len(devices))


class Lane:
    def __init__(self, sends, recvs, base):
        self.sends, self.recvs, self.base, self.out = sends, recvs, base, []

    def send(self, source, target, number, device):
        copy = pltpu.make_async_remote_copy(
            src_ref=source,
            dst_ref=target,
            send_sem=self.sends.at[self.base + number],
            recv_sem=self.recvs.at[self.base + number],
            device_id=device,
            device_id_type=MESH,
        )
        copy.start()
        self.out.append(copy)

    def arrive(self, target, number, device):
        pltpu.make_async_remote_copy(
            src_ref=target,
            dst_ref=target,
            send_sem=self.sends.at[self.base + number],
            recv_sem=self.recvs.at[self.base + number],
            device_id=device,
            device_id_type=MESH,
        ).wait_recv()

    def drain(self):
        for copy in self.out:
            copy.wait_send()
        self.out = []


class Spread(Lane):
    def setup(self, item, plus, minus):
        self.item, self.plus, self.minus = item, plus, minus
        half = item(0).shape[0] // 2
        self.first, self.second = pl.ds(0, half), pl.ds(half, half)
        return self

    def start(self):
        self.send(self.item(0), self.item(0), 0, self.plus)
        self.send(self.item(0), self.item(0), 1, self.minus)

    def relay_up(self):
        block = self.item(-1)
        self.arrive(block, 0, self.minus)
        self.send(block.at[self.first], block.at[self.first], 2, self.plus)

    def relay_down(self):
        block = self.item(1)
        self.arrive(block, 1, self.plus)
        self.send(block.at[self.second], block.at[self.second], 3, self.minus)

    def finish(self):
        block = self.item(2)
        self.arrive(block.at[self.first], 2, self.minus)
        self.arrive(block.at[self.second], 3, self.plus)


class Fold(Lane):
    def setup(self, half_of, land, plus, minus):
        self.half_of, self.land, self.plus, self.minus = half_of, land, plus, minus
        return self

    def start(self):
        self.send(self.half_of(2, 0), self.land.at[0], 0, self.plus)
        self.send(self.half_of(2, 1), self.land.at[1], 1, self.minus)
        self.send(self.half_of(1, 1), self.land.at[3], 3, self.plus)
        self.send(self.half_of(-1, 0), self.land.at[4], 4, self.minus)

    def relay(self):
        self.arrive(self.land.at[0], 0, self.minus)
        combine(self.land.at[0], [self.land.at[0], self.half_of(1, 0)])
        self.send(self.land.at[0], self.land.at[2], 2, self.plus)
        self.arrive(self.land.at[1], 1, self.plus)
        combine(self.land.at[1], [self.land.at[1], self.half_of(-1, 1)])
        self.send(self.land.at[1], self.land.at[5], 5, self.minus)

    def finish(self, totals):
        self.arrive(self.land.at[3], 3, self.minus)
        self.arrive(self.land.at[4], 4, self.plus)
        self.arrive(self.land.at[2], 2, self.minus)
        combine(totals[0], [self.half_of(0, 0), self.land.at[2], self.land.at[4]])
        self.arrive(self.land.at[5], 5, self.plus)
        combine(totals[1], [self.half_of(0, 1), self.land.at[3], self.land.at[5]])


class Detour(Lane):
    def setup(self, item, cuts, land, z, hi, lo):
        self.item, self.cuts, self.land, self.z, self.hi, self.lo = item, cuts, land, z, hi, lo
        side = 2 * lax.rem(z, 2) - 1
        self.at_hi, self.at_lo, self.at_far = wrap(z + side), wrap(z - side), wrap(z + 2)
        return self

    def start(self):
        for n, cut in enumerate(self.cuts):
            self.send(self.item(self.at_far).at[cut], self.land.at[0].at[cut], n, self.hi)
        self.send(self.item(self.at_hi), self.land.at[1], len(self.cuts), self.hi)

    def relay(self, n):
        cut = self.cuts[n]
        passed = self.land.at[0].at[cut]
        self.arrive(passed, n, self.hi)
        combine(passed, [passed, self.item(self.at_lo).at[cut]])
        self.send(passed, self.land.at[2].at[cut], len(self.cuts) + 1 + n, self.lo)

    def finish(self, total):
        self.arrive(self.land.at[1], len(self.cuts), self.hi)
        for n, cut in enumerate(self.cuts):
            self.arrive(self.land.at[2].at[cut], len(self.cuts) + 1 + n, self.lo)
        combine(total, [self.item(self.z), self.land.at[1], self.land.at[2]])


def combine(total, terms):
    lead = total.shape[:-2]

    @pl.loop(0, math.prod(lead))
    def _(n):
        at = []
        for extent in reversed(lead):
            at.append(lax.rem(n, extent))
            n = lax.div(n, extent)
        at = tuple(reversed(at))
        value = terms[0][at].astype(F32)
        for term in terms[1:]:
            value = value + term[at].astype(F32)
        total[at] = value.astype(total.dtype)


def head_columns(z, x):
    return pl.ds(pl.multiple_of((lax.rem(z, 2) * 4 + x * 8) * D, WIDTH), WIDTH)


def pair_table(z, y, x, c, docs, mask, order):
    z_hi = lax.div(z, 2)
    row = lax.broadcasted_iota(jnp.int32, (T, T), 0)
    col = lax.broadcasted_iota(jnp.int32, (T, T), 1)
    doc_cols = jnp.broadcast_to(docs[...].astype(F32), (T, T))
    live = (mask[...] == 1) & (doc_cols.T == doc_cols) & (row >= col)
    live = jnp.where(live, 1.0, 0.0).astype(BF16)
    holds = jnp.where(row == jnp.broadcast_to(order[...], (T, T)), 1.0, 0.0).astype(BF16)
    by_key = jnp.dot(live, holds, preferred_element_type=F32).astype(BF16)
    stored = lax.dot_general(holds, by_key, TN, preferred_element_type=F32).astype(BF16)
    small_row = lax.broadcasted_iota(jnp.int32, (QUERY_TILES, T), 0)
    small_col = lax.broadcasted_iota(jnp.int32, (QUERY_TILES, T), 1)
    first = (z_hi * 4 + y) * QUERY_TILES
    pick = jnp.where(small_col == small_row + first, 1.0, 0.0).astype(BF16)
    mine = jnp.dot(pick, stored, preferred_element_type=F32).astype(BF16)
    slot_z, slot_y, slot_x = col // 16, col // 4 % 4, col % 4
    source = (slot_z // 2) * 64 + slot_y * 16 + c * 8 + slot_z % 2 * 4 + slot_x
    spread = jnp.where((row == source) & (col < KEY_TILES), 1.0, 0.0).astype(BF16)
    pairs = jnp.dot(mine, spread, preferred_element_type=F32)
    own = ((z_hi * 2 + small_row % 8 // 4) * 4 + y) * 4 + small_row % 4
    is_own = (small_col == own) & (small_row // 8 == c)
    diag = jnp.sum(jnp.where(is_own, pairs, 0.0), axis=1, keepdims=True)
    rest = jnp.where(is_own, 0.0, pairs)
    upto = jnp.where(row <= col, 1.0, 0.0).astype(BF16)
    rank = jnp.dot(rest.astype(BF16), upto, preferred_element_type=F32)
    count = jnp.sum(rest, axis=1, keepdims=True)
    numbers = lax.broadcasted_iota(jnp.int32, (8, T), 1).astype(F32).astype(BF16)
    lists = []
    for i in range(QUERY_TILES):
        at = jnp.where(rest[i : i + 1, :] > 0.5, rank[i : i + 1, :] - 1.0, -1.0)
        chosen = jnp.where(jnp.broadcast_to(at, (T, T)) == row.astype(F32), 1.0, 0.0).astype(BF16)
        lists.append(lax.dot_general(numbers, chosen, NT, preferred_element_type=F32)[:1])
    table = jnp.concatenate(lists, axis=0)
    table = jnp.where(small_col == KEY_TILES, count, table)
    table = jnp.where(small_col == KEY_TILES + 1, diag, table)
    table = table.astype(jnp.int32)
    return jnp.where(small_col == KEY_TILES + 2, jnp.where(small_row // 8 == c, own, 0), table)


def gather(
    queries, grad_out, keys, values, attn_in, logs_in, docs_in, mask_in, order_in,
    sibling_rows, kg, vg, stats, table_out,
    table, attn_out, log_sums, docs, mask, order,
    own_grad, stat_parts, sends, recvs, local,
):
    z, y, x, c = place()
    ka = lax.rem(z, 2) * 4 + x
    columns = head_columns(z, x)
    own_rows = pl.ds(pl.multiple_of(ka * T, T), T)
    loads = [
        pltpu.make_async_copy(source, target, local.at[6 + n])
        for n, (source, target) in enumerate(
            (
                (attn_in, attn_out),
                (logs_in, log_sums),
                (docs_in, docs),
                (mask_in, mask),
                (order_in, order),
            )
        )
    ]
    loads.append(pltpu.make_async_copy(grad_out.at[own_rows], own_grad, local.at[0]))
    for copy in loads:
        copy.start()

    def part(ref, to):
        return ref.at[:, pl.ds(pl.multiple_of(to * D, D), D)]

    peers = group_peers(z, y, x, c)
    y_plus, y_minus = ident(z, wrap(y + 1), x, c), ident(z, wrap(y - 1), x, c)
    z_plus, z_minus = ident(wrap(z + 1), y, x, c), ident(wrap(z - 1), y, x, c)
    far = ident(wrap(z + 2 * lax.rem(z, 2) - 1), y, x, c)
    greet([peer for _, _, peer in peers] + [y_plus, y_minus, far])

    slot = pl.ds(pl.multiple_of(x * T, T), T)
    across = Lane(sends, recvs, 0)
    for step in range(1, RING):
        to = wrap(x + step)
        across.send(part(keys, to), kg.at[z, y, slot], step - 1, ident(z, y, to, c))
        across.send(part(values, to), vg.at[z, y, slot], step + 2, ident(z, y, to, c))
    kept = [
        pltpu.make_async_copy(part(keys, x), kg.at[z, y, slot], local.at[3]),
        pltpu.make_async_copy(part(values, x), vg.at[z, y, slot], local.at[4]),
    ]
    for copy in kept:
        copy.start()
    sibling = ident(z, y, x, 1 - c)
    pair = Lane(sends, recvs, 6)
    pair.send(queries.at[:, columns], sibling_rows.at[0], 0, sibling)
    pair.send(grad_out.at[:, columns], sibling_rows.at[1], 1, sibling)

    for copy in kept:
        copy.wait()
    for step in range(1, RING):
        origin = wrap(x - step)
        came = pl.ds(pl.multiple_of(origin * T, T), T)
        across.arrive(kg.at[z, y, came], step - 1, ident(z, y, origin, c))
        across.arrive(vg.at[z, y, came], step + 2, ident(z, y, origin, c))

    def block(ref, dz, dy):
        return ref.at[wrap(z + dz), wrap(y + dy)]

    base = 24
    key_first = Spread(sends, recvs, base).setup(lambda o: block(kg, o, 0), z_plus, z_minus)
    value_first = Spread(sends, recvs, base + 4).setup(lambda o: block(vg, 0, o), y_plus, y_minus)
    key_then, value_then = {}, {}
    for n, off in enumerate((0, -1, 1, 2)):
        key_then[off] = Spread(sends, recvs, base + 8 + 4 * n).setup(
            lambda o, off=off: block(kg, off, o), y_plus, y_minus
        )
        value_then[off] = Spread(sends, recvs, base + 24 + 4 * n).setup(
            lambda o, off=off: block(vg, o, off), z_plus, z_minus
        )
    key_first.start()
    value_first.start()
    key_then[0].start()
    value_then[0].start()

    for copy in loads:
        copy.wait()
    for to in range(KA):
        first = to % 4 * 8 + to // 4 * 4
        stat_parts[to, 0:HEADS, :] = log_sums[first : first + HEADS, :]
        for h in range(HEADS):
            lanes = pl.ds((first + h) * D, D)
            product = own_grad[:, lanes].astype(F32) * attn_out[:, lanes].astype(F32)
            stat_parts[to, HEADS + h : HEADS + h + 1, :] = jnp.sum(product.T, axis=0, keepdims=True)
    share = Lane(sends, recvs, 8)
    for flip, step, peer in peers:
        share.send(stat_parts.at[lax.rem(ka + step, KA)], stats.at[c * KA + ka], flip * KA + step, peer)
    keep_stats = pltpu.make_async_copy(stat_parts.at[ka], stats.at[c * KA + ka], local.at[5])
    keep_stats.start()

    key_first.relay_up()
    value_first.relay_up()
    key_then[-1].start()
    value_then[-1].start()
    key_first.relay_down()
    value_first.relay_down()
    key_then[1].start()
    value_then[1].start()
    table[...] = pair_table(z, y, x, c, docs, mask, order)
    keep_table = pltpu.make_async_copy(table, table_out, local.at[11])
    keep_table.start()
    for off in (0,):
        key_then[off].relay_up()
        value_then[off].relay_up()
        key_then[off].relay_down()
        value_then[off].relay_down()
    key_first.finish()
    value_first.finish()
    key_then[2].start()
    value_then[2].start()
    for off in (-1, 1, 2):
        key_then[off].relay_up()
        value_then[off].relay_up()
        key_then[off].relay_down()
        value_then[off].relay_down()
    for off in (0, -1, 1, 2):
        key_then[off].finish()
        value_then[off].finish()

    pair.arrive(sibling_rows.at[0], 0, sibling)
    pair.arrive(sibling_rows.at[1], 1, sibling)
    for flip, step, _ in peers:
        origin = lax.rem(ka + KA - step, KA)
        core = 1 - c if flip else c
        from_ = ident(lax.div(z, 2) * 2 + lax.div(origin, 4), y, lax.rem(origin, 4), core)
        share.arrive(stats.at[core * KA + origin], flip * KA + step, from_)
    keep_stats.wait()
    keep_table.wait()
    for lane in [across, pair, share, key_first, value_first, *key_then.values(), *value_then.values()]:
        lane.drain()


def attend(
    table, stats_in, queries, grad_out, sibling_rows, keys_in, values_in, key_gain, value_gain,
    dq_ref, dk_ref, dv_ref, gains,
    plan, stats, q_ref, g_ref, keys, values, k_ref, v_ref, dk_acc, dv_acc, dq_acc, held, gain_acc, local,
):
    scale = D ** -0.5
    z, _, x, c = place()
    columns = head_columns(z, x)
    own, other = [pl.ds(pl.multiple_of(core * KA * T, KA * T), KA * T) for core in (c, 1 - c)]
    loads = [
        pltpu.make_async_copy(source, target, local.at[n])
        for n, (source, target) in enumerate(
            (
                (keys_in, keys),
                (values_in, values),
                (stats_in, stats),
                (queries.at[:, columns], q_ref.at[own]),
                (grad_out.at[:, columns], g_ref.at[own]),
                (sibling_rows.at[0], q_ref.at[other]),
                (sibling_rows.at[1], g_ref.at[other]),
            )
        )
    ]
    for copy in loads:
        copy.start()
    dk_acc[...] = jnp.zeros_like(dk_acc)
    dv_acc[...] = jnp.zeros_like(dv_acc)
    dq_acc[...] = jnp.zeros_like(dq_acc)

    def stack(ref, i):
        rows = pl.ds(pl.multiple_of(i * T, T), T)
        return jnp.concatenate([ref[rows, h * D : (h + 1) * D] for h in range(HEADS)], axis=0)

    def tiles(ref, a, b):
        parts = [ref[pl.ds(pl.multiple_of(at * T, T), T), :] for at in (a, b)]
        return jnp.concatenate(parts, axis=0)

    def unpack(step):
        word = plan[step]
        return word >> 16, (word >> 8) & 63, word & 63, (word >> 14) & 1, (word >> 6) & 1

    def front(step, slot, masked):
        i, a, b, use_a, use_b = unpack(step)
        s = lax.dot_general(tiles(k_ref, a, b), stack(q_ref, i), NT, preferred_element_type=F32)
        dp = lax.dot_general(tiles(v_ref, a, b), stack(g_ref, i), NT, preferred_element_type=F32)
        lse = jnp.concatenate([stats[i, h : h + 1, :] for h in range(HEADS)], axis=1) * LOG2E
        delta = jnp.concatenate([stats[i, HEADS + h : HEADS + h + 1, :] for h in range(HEADS)], axis=1)
        p = jnp.exp2(s * (scale * LOG2E) - lse)
        if masked:
            row = lax.broadcasted_iota(jnp.int32, (T, T), 0)
            col = lax.broadcasted_iota(jnp.int32, (T, T), 1)
            ok_a = row < use_a * T
            ok_b = row <= col - (1 - use_b) * T
            ok = jnp.concatenate(
                [jnp.concatenate([ok_a] * HEADS, axis=1), jnp.concatenate([ok_b] * HEADS, axis=1)], axis=0
            )
            p = jnp.where(ok, p, 0.0)
        held[slot, 0] = p.astype(BF16)
        held[slot, 1] = (p * (dp - delta)).astype(BF16)

    def back(step, slot):
        i, a, b, _, _ = unpack(step)
        p, ds = held[slot, 0], held[slot, 1]
        dv = jnp.dot(p, stack(g_ref, i), preferred_element_type=F32)
        dk = jnp.dot(ds, stack(q_ref, i), preferred_element_type=F32)
        dq_acc[i] += lax.dot_general(tiles(k_ref, a, b), ds, TN, preferred_element_type=F32)
        for n, at in enumerate((a, b)):
            rows = pl.ds(pl.multiple_of(at * T, T), T)
            dv_acc[rows, :] += dv[n * T : (n + 1) * T]
            dk_acc[rows, :] += dk[n * T : (n + 1) * T]

    def run(steps, masked, unroll):
        plan[steps] = 0
        front(0, 0, masked)

        def twos(first, count):
            for r in range(0, count, 2):
                front(first + r + 1, 1, masked)
                back(first + r, 0)
                front(first + r + 2, 0, masked)
                back(first + r + 1, 1)

        whole = lax.div(steps, unroll)

        @pl.loop(0, whole)
        def _(u):
            twos(u * unroll, unroll)

        if unroll > 2:

            @pl.loop(whole * (unroll // 2), lax.div(steps, 2))
            def _(u):
                twos(2 * u, 2)

        @pl.when(lax.rem(steps, 2) > 0)
        def _():
            back(steps - 1, 0)

    def list_whole(i, n):
        halves = lax.div(table[i, KEY_TILES], 2)

        def put(r, n):
            plan[n] = (i << 16) | (table[i, 2 * r] << 8) | table[i, 2 * r + 1]
            return n + 1

        return lax.fori_loop(0, halves, put, n)

    steps = lax.fori_loop(0, QUERY_TILES, list_whole, jnp.int32(0))
    lanes = pl.ds(pl.multiple_of(x * D, D), D)
    for n, (raw, scaled, gain) in enumerate(((keys, k_ref, key_gain), (values, v_ref, value_gain))):
        loads[n].wait()
        factor = gain[:, lanes]

        @pl.loop(0, KEY_TILES // 2)
        def _(n):
            at = pl.ds(pl.multiple_of(n * 2 * T, 2 * T), 2 * T)
            scaled[at, :] = (raw[at, :].astype(F32) * factor).astype(BF16)

    for copy in loads[2:]:
        copy.wait()
    run(steps, False, 8)

    def list_masked(i, n):
        count, diag = table[i, KEY_TILES], table[i, KEY_TILES + 1]
        odd = lax.rem(count, 2)
        last = table[i, jnp.maximum(count - 1, 0)]

        @pl.when(odd + diag > 0)
        def _():
            plan[n] = (i << 16) | (odd << 14) | (last << 8) | (diag << 6) | table[i, KEY_TILES + 2]

        return n + jnp.minimum(odd + diag, 1)

    run(lax.fori_loop(0, QUERY_TILES, list_masked, jnp.int32(0)), True, 4)

    @pl.loop(0, QUERY_TILES)
    def _(i):
        rows = pl.ds(pl.multiple_of(i * T, T), T)
        for h in range(HEADS):
            lanes = slice(h * D, (h + 1) * D)
            dq_ref[rows, lanes] = (dq_acc[i, :, lanes] * scale).astype(BF16).T

    gain_acc[...] = jnp.zeros_like(gain_acc)

    @pl.loop(0, KEY_TILES)
    def _(n):
        at = pl.ds(pl.multiple_of(n * T, T), T)
        dkey, dvalue = dk_acc[at, :] * scale, dv_acc[at, :]
        owner = (lax.div(n, 16), lax.rem(lax.div(n, 4), 4), lax.rem(n, 4))
        dk_ref[owner] = dkey.astype(BF16)
        dv_ref[owner] = dvalue.astype(BF16)
        gain_acc[0] += jnp.sum((dkey * keys[at, :].astype(F32)).reshape(T // 8, 8, D), axis=0)
        gain_acc[1] += jnp.sum((dvalue * values[at, :].astype(F32)).reshape(T // 8, 8, D), axis=0)

    gains[...] = jnp.zeros_like(gains)
    for n in range(2):
        gains[n : n + 1, :] = jnp.sum(gain_acc[n], axis=0, keepdims=True)


def scatter(
    dq, dk, dv, partial, key_gain, value_gain,
    grad_queries, grad_keys, grad_values, grad_key_gain, grad_value_gain,
    dq_in, land_z, land_v, land_k, out_k, out_v, in_k, in_v, near, total, sends, recvs,
):
    z, y, x, c = place()
    ka = lax.rem(z, 2) * 4 + x
    z_hi, z_lo = lax.div(z, 2), lax.rem(z, 2)
    y_plus, y_minus = ident(z, wrap(y + 1), x, c), ident(z, wrap(y - 1), x, c)
    z_far, z_near = ident(wrap(z + 2 * z_lo - 1), y, x, c), ident(wrap(z + 1 - 2 * z_lo), y, x, c)
    steps = [(one, two) for one in range(RING) for two in range(RING) if one or two]
    in_y = [ident(z, wrap(y + one), wrap(x + two), c) for one, two in steps]
    in_z = [ident(wrap(z + one), y, wrap(x + two), c) for one, two in steps]
    others = [(0, one, ident(wrap(z + one), y, x, c)) for one in range(1, RING)]
    others += [(1, one, ident(wrap(z + one), y, x, 1 - c)) for one in range(RING)]
    greet(in_y + [peer for peer, (one, _) in zip(in_z, steps) if one] + [other for flip, _, other in others if flip])

    spread = Lane(sends, recvs, 56)
    for (one, two), peer in zip(steps, in_y):
        spread.send(partial, near.at[one, two], one * RING + two, peer)
    near[0, 0] = partial[...]

    sibling = ident(z, y, x, 1 - c)
    pair = Lane(sends, recvs, 0)
    for n in range(KA):
        to = lax.rem(ka + n + 1, KA)
        rows = pl.ds(pl.multiple_of(((1 - c) * KA + to) * T, T), T)
        pair.send(dq.at[rows], dq_in.at[to], n, sibling)

    keys_z = Detour(sends, recvs, 16).setup(
        lambda at: dk.at[at, :, pl.ds(0, Z_FIRST)], [pl.ds(0, 2), pl.ds(2, 2)], land_z, z, z_far, z_near
    )
    last_y = Fold(sends, recvs, 22).setup(
        lambda off, n: dk.at[pl.ds(2 * n, 2), wrap(y + off), pl.ds(Z_FIRST, RING - Z_FIRST)], land_k, y_plus, y_minus
    )
    rows_of = [pl.ds(n * (T // PARTS), T // PARTS) for n in range(PARTS)]
    values_y = [
        Fold(sends, recvs, 72 + 22 * part).setup(
            lambda off, n, rows=rows: dv.at[pl.ds(2 * n, 2), wrap(y + off), :, rows], land_v.at[part], y_plus, y_minus
        )
        for part, rows in enumerate(rows_of)
    ]
    keys_z.start()
    last_y.start()
    for lane in values_y:
        lane.start()

    lane_q = Lane(sends, recvs, 8)
    columns = head_columns(z, x)
    for n in range(KA):
        to = lax.rem(ka + n + 1, KA)
        own_rows = dq.at[pl.ds(pl.multiple_of((c * KA + to) * T, T), T)]
        pair.arrive(dq_in.at[to], n, sibling)
        for h in range(HEADS):
            lanes = pl.ds(h * D, D)
            value = own_rows[:, lanes].astype(F32) + dq_in[to, :, lanes].astype(F32)
            dq_in[to, :, lanes] = value.astype(BF16)
        if n < KA - 1:
            peer = ident(z_hi * 2 + lax.div(to, 4), y, lax.rem(to, 4), c)
            lane_q.send(dq_in.at[to], grad_queries.at[:, columns], n + 1, peer)
    grad_queries[:, columns] = dq_in[ka]

    for (one, two), peer in zip(steps, in_y):
        spread.arrive(near.at[one, two], one * RING + two, peer)
    for n in range(RING):
        block = near[wrap(y), wrap(x - n + RING)]
        for one in range(1, RING):
            block = block + near[wrap(y - one + RING), wrap(x - n + RING)]
        total[0, 2 * n : 2 * n + 2, :] = block[0:2]
    mine = c * RING + z
    total[1 + mine] = total[0]
    share = Lane(sends, recvs, 28)
    for flip, step, other in others:
        share.send(total.at[0], total.at[1 + mine], flip * RING + step, other)

    def finish_values(part):
        values_y[part].finish([out_v.at[pl.ds(2 * n, 2), :, rows_of[part]] for n in range(2)])

    last_y.relay()
    keys_z.relay(0)
    values_y[0].relay()
    keys_z.relay(1)
    last_y.finish([out_k.at[pl.ds(2 * n, 2), pl.ds(Z_FIRST, RING - Z_FIRST)] for n in range(2)])
    finish_values(0)

    def send_values(part):
        lane = Lane(sends, recvs, 78 + 22 * part)
        for (one, two), peer in zip(steps, in_z):
            block = out_v.at[wrap(z + one), wrap(x + two), rows_of[part]]
            lane.send(block, in_v.at[one, two, rows_of[part]], one * RING + two, peer)
        return lane

    values_out = [send_values(0)]
    for part in range(1, PARTS):
        values_y[part].relay()
        finish_values(part)
        values_out.append(send_values(part))
    keys_z.finish(out_k.at[:, pl.ds(0, Z_FIRST)])
    keys_out = Lane(sends, recvs, 40)
    for one, two in steps:
        to = wrap(x + two)
        over_z = lax.div(to, Z_FIRST)
        to_z, to_y = wrap(z + one * over_z), wrap(y + one * (1 - over_z))
        block = out_k.at[over_z * to_z + (1 - over_z) * to_y, to]
        keys_out.send(block, in_k.at[one, two], one * RING + two, ident(to_z, to_y, to, c))

    def deliver(result, gain, own, came):
        for two in range(RING):
            lanes = pl.ds(pl.multiple_of(wrap(x - two) * D, D), D)
            value = (own if two == 0 else came[0, two]).astype(F32)
            for one in range(1, RING):
                value = value + came[one, two].astype(F32)
            result[:, lanes] = (value * gain[:, lanes]).astype(BF16)

    for (one, two), peer in zip(steps, in_y):
        keys_out.arrive(in_k.at[one, two], one * RING + two, peer)
    own_over_z = lax.div(x, Z_FIRST)
    deliver(grad_keys, key_gain, out_k[own_over_z * z + (1 - own_over_z) * y, x], in_k)
    for part in range(PARTS):
        for (one, two), peer in zip(steps, in_z):
            values_out[part].arrive(in_v.at[one, two, rows_of[part]], one * RING + two, peer)
    deliver(grad_values, value_gain, out_v[z, x], in_v)

    for flip, step, other in others:
        origin = (1 - c if flip else c) * RING + wrap(z - step)
        share.arrive(total.at[1 + origin], flip * RING + step, other)
    whole = jnp.sum(total[1:], axis=0)
    for n in range(RING):
        grad_key_gain[:, n * D : (n + 1) * D] = whole[2 * n : 2 * n + 1]
        grad_value_gain[:, n * D : (n + 1) * D] = whole[2 * n + 1 : 2 * n + 2]
    for n in range(1, KA):
        origin = lax.rem(ka + KA - n, KA)
        their = head_columns(lax.div(origin, 4), lax.rem(origin, 4))
        from_ = ident(z_hi * 2 + lax.div(origin, 4), y, lax.rem(origin, 4), c)
        lane_q.arrive(grad_queries.at[:, their], n, from_)
    for lane in [
        pair, lane_q, keys_z, last_y, *values_y, keys_out, *values_out, share, spread
    ]:
        lane.drain()


def shape(dims, dtype):
    return jax.ShapeDtypeStruct(dims, dtype)


def attend_call(table, stats, queries, grad_out, sibling_rows, k, v, key_gain, value_gain):
    vm, hbm = pl.BlockSpec(memory_space=pltpu.VMEM), pl.BlockSpec(memory_space=pl.ANY)
    return pl.pallas_call(
        attend,
        out_shape=(shape((2 * KA * T, WIDTH), BF16), *[shape((RING, RING, RING, T, D), BF16)] * 2, shape((8, D), F32)),
        in_specs=[pl.BlockSpec(memory_space=pltpu.SMEM)] + [hbm] * 6 + [vm] * 2,
        out_specs=(vm,) * 4,
        scratch_shapes=[
            pltpu.SMEM((QUERY_TILES * KEY_TILES // 2 + 2,), jnp.int32),
            pltpu.VMEM(stats.shape, F32),
            pltpu.VMEM((2 * KA * T, WIDTH), BF16),
            pltpu.VMEM((2 * KA * T, WIDTH), BF16),
            pltpu.VMEM(k.shape, BF16),
            pltpu.VMEM(v.shape, BF16),
            pltpu.VMEM(k.shape, BF16),
            pltpu.VMEM(v.shape, BF16),
            pltpu.VMEM(k.shape, F32),
            pltpu.VMEM(v.shape, F32),
            pltpu.VMEM((QUERY_TILES, D, WIDTH), F32),
            pltpu.VMEM((2, 2, 2 * T, WIDTH), BF16),
            pltpu.VMEM((2, 8, D), F32),
            pltpu.SemaphoreType.DMA((7,)),
        ],
        compiler_params=pltpu.CompilerParams(vmem_limit_bytes=47 * 2**20),
        name="attend",
    )(table, stats, queries, grad_out, sibling_rows, k, v, key_gain, value_gain)


def shards(
    queries, key_rows, values, attn_out, grad_out, log_sums, key_gain, value_gain, doc_ids, tile_mask, block_order
):
    vm, hbm = pl.BlockSpec(memory_space=pltpu.VMEM), pl.BlockSpec(memory_space=pl.ANY)
    key_gain, value_gain = key_gain.reshape(1, -1), value_gain.reshape(1, -1)
    rows = queries.shape[0]
    sibling_rows, kg, vg, stats, table = pl.pallas_call(
        gather,
        out_shape=(
            shape((2, rows, WIDTH), BF16),
            shape((RING, RING, RING * T, D), BF16),
            shape((RING, RING, RING * T, D), BF16),
            shape((QUERY_TILES, 2 * HEADS, T), F32),
            shape((QUERY_TILES, T), jnp.int32),
        ),
        in_specs=[hbm] * 9,
        out_specs=(hbm,) * 5,
        scratch_shapes=[
            pltpu.VMEM((QUERY_TILES, T), jnp.int32),
            pltpu.VMEM(attn_out.shape, BF16),
            pltpu.VMEM(log_sums.shape, F32),
            pltpu.VMEM((1, T), jnp.int32),
            pltpu.VMEM(tile_mask.shape, jnp.int32),
            pltpu.VMEM((1, T), jnp.int32),
            pltpu.VMEM(attn_out.shape, BF16),
            pltpu.VMEM((KA, 2 * HEADS, T), F32),
            pltpu.SemaphoreType.DMA((64,)),
            pltpu.SemaphoreType.DMA((64,)),
            pltpu.SemaphoreType.DMA((12,)),
        ],
        compiler_params=pltpu.CompilerParams(
            collective_id=0, has_side_effects=True, vmem_limit_bytes=56 * 2**20
        ),
        name="gather",
    )(
        queries, grad_out, key_rows, values, attn_out, log_sums,
        doc_ids.reshape(1, -1), tile_mask, block_order.reshape(1, -1),
    )
    dq, dk, dv, partial = attend_call(
        table, stats, queries, grad_out, sibling_rows,
        kg.reshape(KEY_TILES * T, D), vg.reshape(KEY_TILES * T, D), key_gain, value_gain,
    )
    grad_queries, grad_keys, grad_values, grad_key_gain, grad_value_gain = pl.pallas_call(
        scatter,
        out_shape=(
            shape(attn_out.shape, BF16),
            shape(key_rows.shape, BF16),
            shape(values.shape, BF16),
            shape(key_gain.shape, F32),
            shape(value_gain.shape, F32),
        ),
        in_specs=[vm] * 6,
        out_specs=(vm,) * 5,
        scratch_shapes=[
            pltpu.VMEM((KA, T, WIDTH), BF16),
            pltpu.VMEM((3, RING, Z_FIRST, T, D), BF16),
            pltpu.VMEM((PARTS, 6, 2, RING, T // PARTS, D), BF16),
            pltpu.VMEM((6, 2, RING - Z_FIRST, T, D), BF16),
            pltpu.VMEM((RING, RING, T, D), BF16),
            pltpu.VMEM((RING, RING, T, D), BF16),
            pltpu.VMEM((RING, RING, T, D), BF16),
            pltpu.VMEM((RING, RING, T, D), BF16),
            pltpu.VMEM((RING, RING, 8, D), F32),
            pltpu.VMEM((9, 8, D), F32),
            pltpu.SemaphoreType.DMA((72 + 22 * PARTS,)),
            pltpu.SemaphoreType.DMA((72 + 22 * PARTS,)),
        ],
        compiler_params=pltpu.CompilerParams(
            collective_id=1, has_side_effects=True, vmem_limit_bytes=20 * 2**20
        ),
        name="scatter",
    )(dq, dk, dv, partial, key_gain, value_gain)
    return grad_queries, grad_keys, grad_values, grad_key_gain.reshape(-1), grad_value_gain.reshape(-1)


def solution(mesh):
    rows = P(("pb", "ka"), None)
    placed = (P("pb", None), rows, rows, rows, P("pb", None), P(None, ("pb", "ka")), P(), P(), P(), P(), P())
    return jax.shard_map(
        shards, mesh=mesh, in_specs=placed, out_specs=(rows, rows, rows, P(), P()), check_vma=False
    )
```

profile of v0, /device:TPU:1, one launch (start us, length us, event | category | flops | bytes accessed | tf_op | source)
XLA Modules:
  0.0 129.8 jit_solution(911423284080882020)
XLA Ops:
  0.6 0.0 copy-start.2
  0.6 0.0 copy-start.3
  0.7 36.4 %gather.1 = (bf16[2,1024,512]{2,1,0:T(8,128)(2,1)}, bf16[4,4,512,128]{3,2,1,0:T(8,128)(2,1)}, bf16[4,4,512,128]{3,2,1,0:T(8,128)(2,1)}, f32[16,8,128]{2,1,0:T(8,128)}, s32[16,128]{1,0:T(8,128)}) custom-call(bf16[1024,4096]{1,0:T(8,128)(2,1)} %queries.3, bf16[1024,4096]{1,0:T(8,128)(2,1)} %grad_out.3, bf16[128,512]{1,0:T(8,128)(2,1)} %keys.1, ...), custom_call_target="tpu_custom_call" | custom-call | tf_op jit(solution)/shard_map/gather/pallas_call | solution.py:709
  37.1 0.0 copy-done.2
  37.1 0.0 copy-done.3
  37.1 0.0 copy-start
  37.1 0.8 copy-done
  37.9 0.0 copy-start.1
  37.9 0.7 copy-done.1
  38.6 36.4 %attend.1 = (bf16[2048,512]{1,0:T(8,128)(2,1)S(1)}, bf16[4,4,4,128,128]{4,3,2,1,0:T(8,128)(2,1)S(1)}, bf16[4,4,4,128,128]{4,3,2,1,0:T(8,128)(2,1)S(1)}, f32[8,128]{1,0:T(8,128)S(1)}) custom-call(s32[16,128]{1,0:T(8,128)S(1)} %copy-done.1, f32[16,8,128]{2,1,0:T(8,128)S(1)} %copy-done, bf16[1024,4096]{1,0:T(8,128)(2,1)} %queries.3, ...), custom_call_target="tpu_custom_call" | custom-call | tf_op jit(solution)/shard_map/attend/pallas_call | solution.py:677
  75.1 51.3 %scatter.1 = (bf16[128,4096]{1,0:T(8,128)(2,1)S(1)}, bf16[128,512]{1,0:T(8,128)(2,1)S(1)}, bf16[128,512]{1,0:T(8,128)(2,1)S(1)}, f32[1,512]{1,0:T(1,128)S(1)}, f32[1,512]{1,0:T(1,128)S(1)}) custom-call(bf16[2048,512]{1,0:T(8,128)(2,1)S(1)} %get-tuple-element.24.dq, bf16[4,4,4,128,128]{4,3,2,1,0:T(8,128)(2,1)S(1)} %get-tuple-element.25.dk, ...), custom_call_target="tpu_custom_call" | custom-call | tf_op jit(solution)/shard_map/scatter/pallas_call | solution.py:745
  126.4 1.0 copy.21
  127.4 0.7 copy.22
  128.0 0.7 copy.23
  128.7 0.6 copy.24
  129.3 0.6 copy.25
Async XLA Ops:
  0.6 36.4 %copy-start.2 = (f32[512]{0:T(512)S(1)}, f32[512]{0:T(512)}, u32[]{:S(2)}) copy-start(f32[512]{0:T(512)} %param.17) | copy-start | bytes 6148
  0.6 36.4 %copy-start.3 = (f32[512]{0:T(512)S(1)}, f32[512]{0:T(512)}, u32[]{:S(2)}) copy-start(f32[512]{0:T(512)} %param.18) | copy-start | bytes 6148
  37.1 0.8 copy-start
  37.9 0.7 copy-start.1
where the time goes:
time: 130 us
  Pallas kernels  124 us (95%)
  local copies, waits for them, and re-layouts  4.98 us (4%)
    pallas_call x1, Pallas kernels, shards(): pl.pallas_call(scatter, out_shape=(shape(attn_out.shape, BF16), shape(key...  51.3 us
    pallas_call x1, Pallas kernels, attend_call(): pl.pallas_call(attend, out_shape=(shape((2 * KA * T, WIDTH), BF16), *[sha...  36.4 us
    pallas_call x1, Pallas kernels, shards(): pl.pallas_call(gather, out_shape=(shape((2, rows, WIDTH), BF16), shape((R...  36.4 us
    unnamed x13, local copies, waits for them, and re-layouts  4.98 us

commit v1 on v0

--- a/solution.py
+++ b/solution.py
@@ -401,81 +401,95 @@
         rows = pl.ds(pl.multiple_of(i * T, T), T)
         return jnp.concatenate([ref[rows, h * D : (h + 1) * D] for h in range(HEADS)], axis=0)
 
-    def tiles(ref, a, b):
-        parts = [ref[pl.ds(pl.multiple_of(at * T, T), T), :] for at in (a, b)]
-        return jnp.concatenate(parts, axis=0)
-
-    def unpack(step):
+    def tiles(ref, places):
+        parts = [ref[pl.ds(pl.multiple_of(at * T, T), T), :] for at in places]
+        return parts[0] if len(parts) == 1 else jnp.concatenate(parts, axis=0)
+
+    def unpack(step, width):
         word = plan[step]
-        return word >> 16, (word >> 8) & 63, word & 63, (word >> 14) & 1, (word >> 6) & 1
-
-    def front(step, slot, masked):
-        i, a, b, use_a, use_b = unpack(step)
-        s = lax.dot_general(tiles(k_ref, a, b), stack(q_ref, i), NT, preferred_element_type=F32)
-        dp = lax.dot_general(tiles(v_ref, a, b), stack(g_ref, i), NT, preferred_element_type=F32)
+        places = ((word >> 8) & 63, word & 63)
+        return word >> 16, places[2 - width :], (word >> 6) & 1
+
+    def front(step, slot, masked, width):
+        i, places, diag = unpack(step, width)
+        s = lax.dot_general(tiles(k_ref, places), stack(q_ref, i), NT, preferred_element_type=F32)
+        dp = lax.dot_general(tiles(v_ref, places), stack(g_ref, i), NT, preferred_element_type=F32)
         lse = jnp.concatenate([stats[i, h : h + 1, :] for h in range(HEADS)], axis=1) * LOG2E
         delta = jnp.concatenate([stats[i, HEADS + h : HEADS + h + 1, :] for h in range(HEADS)], axis=1)
         p = jnp.exp2(s * (scale * LOG2E) - lse)
         if masked:
             row = lax.broadcasted_iota(jnp.int32, (T, T), 0)
             col = lax.broadcasted_iota(jnp.int32, (T, T), 1)
-            ok_a = row < use_a * T
-            ok_b = row <= col - (1 - use_b) * T
-            ok = jnp.concatenate(
-                [jnp.concatenate([ok_a] * HEADS, axis=1), jnp.concatenate([ok_b] * HEADS, axis=1)], axis=0
-            )
-            p = jnp.where(ok, p, 0.0)
-        held[slot, 0] = p.astype(BF16)
-        held[slot, 1] = (p * (dp - delta)).astype(BF16)
-
-    def back(step, slot):
-        i, a, b, _, _ = unpack(step)
-        p, ds = held[slot, 0], held[slot, 1]
+            ok = jnp.concatenate([row <= col + (1 - diag) * T] * HEADS, axis=1)
+            last = jnp.where(ok, p[-T:], 0.0)
+            p = last if width == 1 else jnp.concatenate([p[:T], last], axis=0)
+        rows = slice(0, width * T)
+        held[slot, 0, rows] = p.astype(BF16)
+        held[slot, 1, rows] = (p * (dp - delta)).astype(BF16)
+
+    def back(step, slot, width):
+        i, places, _ = unpack(step, width)
+        rows = slice(0, width * T)
+        p, ds = held[slot, 0, rows], held[slot, 1, rows]
         dv = jnp.dot(p, stack(g_ref, i), preferred_element_type=F32)
         dk = jnp.dot(ds, stack(q_ref, i), preferred_element_type=F32)
-        dq_acc[i] += lax.dot_general(tiles(k_ref, a, b), ds, TN, preferred_element_type=F32)
-        for n, at in enumerate((a, b)):
+        dq_acc[i] += lax.dot_general(tiles(k_ref, places), ds, TN, preferred_element_type=F32)
+        for n, at in enumerate(places):
             rows = pl.ds(pl.multiple_of(at * T, T), T)
             dv_acc[rows, :] += dv[n * T : (n + 1) * T]
             dk_acc[rows, :] += dk[n * T : (n + 1) * T]
 
-    def run(steps, masked, unroll):
-        plan[steps] = 0
-        front(0, 0, masked)
+    def run(base, steps, masked, width, unroll):
+        @pl.when(steps > 0)
+        def _():
+            plan[base + steps] = 0
+            front(base, 0, masked, width)
 
         def twos(first, count):
             for r in range(0, count, 2):
-                front(first + r + 1, 1, masked)
-                back(first + r, 0)
-                front(first + r + 2, 0, masked)
-                back(first + r + 1, 1)
-
-        whole = lax.div(steps, unroll)
-
-        @pl.loop(0, whole)
+                at = base + first + r
+                front(at + 1, 1, masked, width)
+                back(at, 0, width)
+                front(at + 2, 0, masked, width)
+                back(at + 1, 1, width)
+
+        rounds = lax.div(steps, unroll)
+
+        @pl.loop(0, rounds)
         def _(u):
             twos(u * unroll, unroll)
 
         if unroll > 2:
 
-            @pl.loop(whole * (unroll // 2), lax.div(steps, 2))
+            @pl.loop(rounds * (unroll // 2), lax.div(steps, 2))
             def _(u):
                 twos(2 * u, 2)
 
         @pl.when(lax.rem(steps, 2) > 0)
         def _():
-            back(steps - 1, 0)
-
-    def list_whole(i, n):
-        halves = lax.div(table[i, KEY_TILES], 2)
+            back(base + steps - 1, 0, width)
+
+    base_both = QUERY_TILES * KEY_TILES // 2 + 1
+    base_one = base_both + QUERY_TILES + 1
+
+    def list_tile(i, counts):
+        whole, both, one = counts
+        count, diag = table[i, KEY_TILES], table[i, KEY_TILES + 1]
 
         def put(r, n):
             plan[n] = (i << 16) | (table[i, 2 * r] << 8) | table[i, 2 * r + 1]
             return n + 1
 
-        return lax.fori_loop(0, halves, put, n)
-
-    steps = lax.fori_loop(0, QUERY_TILES, list_whole, jnp.int32(0))
+        whole = lax.fori_loop(0, lax.div(count, 2), put, whole)
+        odd = lax.rem(count, 2)
+        left = table[i, jnp.maximum(count - 1, 0)]
+        own = table[i, KEY_TILES + 2]
+        at = jnp.where(odd + diag == 2, base_both + both, base_one + one)
+        plan[at] = (i << 16) | (left << 8) | (diag << 6) | (own * diag + left * (1 - diag))
+        return whole, both + odd * diag, one + jnp.where(odd + diag == 1, 1, 0)
+
+    zero = jnp.int32(0)
+    whole, both, one = lax.fori_loop(0, QUERY_TILES, list_tile, (zero, zero, zero))
     lanes = pl.ds(pl.multiple_of(x * D, D), D)
     for n, (raw, scaled, gain) in enumerate(((keys, k_ref, key_gain), (values, v_ref, value_gain))):
         loads[n].wait()
@@ -488,20 +502,9 @@
 
     for copy in loads[2:]:
         copy.wait()
-    run(steps, False, 8)
-
-    def list_masked(i, n):
-        count, diag = table[i, KEY_TILES], table[i, KEY_TILES + 1]
-        odd = lax.rem(count, 2)
-        last = table[i, jnp.maximum(count - 1, 0)]
-
-        @pl.when(odd + diag > 0)
-        def _():
-            plan[n] = (i << 16) | (odd << 14) | (last << 8) | (diag << 6) | table[i, KEY_TILES + 2]
-
-        return n + jnp.minimum(odd + diag, 1)
-
-    run(lax.fori_loop(0, QUERY_TILES, list_masked, jnp.int32(0)), True, 4)
+    run(0, whole, False, 2, 8)
+    run(base_both, both, True, 2, 4)
+    run(base_one, one, True, 1, 4)
 
     @pl.loop(0, QUERY_TILES)
     def _(i):
@@ -680,7 +683,7 @@
         in_specs=[pl.BlockSpec(memory_space=pltpu.SMEM)] + [hbm] * 6 + [vm] * 2,
         out_specs=(vm,) * 4,
         scratch_shapes=[
-            pltpu.SMEM((QUERY_TILES * KEY_TILES // 2 + 2,), jnp.int32),
+            pltpu.SMEM((QUERY_TILES * KEY_TILES // 2 + 2 * QUERY_TILES + 4,), jnp.int32),
             pltpu.VMEM(stats.shape, F32),
             pltpu.VMEM((2 * KA * T, WIDTH), BF16),
             pltpu.VMEM((2 * KA * T, WIDTH), BF16),

time: 130 us -> 126 us (0.969)
  the two profiles are of different devices: /device:TPU:1 before, /device:TPU:32 now
where the time goes in v1:
time: 126 us; the launch traced here: 127 us
  Pallas kernels  121 us (96%)
  local copies, waits for them, and re-layouts  4.98 us (4%)
    pallas_call x1, Pallas kernels, shards(): pl.pallas_call(scatter, out_shape=(shape(attn_out.shape, BF16), shape(key...  47.1 us
    pallas_call x1, Pallas kernels, shards(): pl.pallas_call(gather, out_shape=(shape((2, rows, WIDTH), BF16), shape((R...  37.3 us
    pallas_call x1, Pallas kernels, attend_call(): pl.pallas_call(attend, out_shape=(shape((2 * KA * T, WIDTH), BF16), *[sha...  36.6 us
    unnamed x13, local copies, waits for them, and re-layouts  4.98 us

profile of v1, /device:TPU:32, one launch (start us, length us, event | category | flops | bytes accessed | tf_op | source)
XLA Modules:
  0.0 126.7 jit_solution(10881008565324061844)
XLA Ops:
  0.6 0.0 copy-start.2
  0.6 0.0 copy-start.3
  0.7 37.3 %gather.1 = (bf16[2,1024,512]{2,1,0:T(8,128)(2,1)}, bf16[4,4,512,128]{3,2,1,0:T(8,128)(2,1)}, bf16[4,4,512,128]{3,2,1,0:T(8,128)(2,1)}, f32[16,8,128]{2,1,0:T(8,128)}, s32[16,128]{1,0:T(8,128)}) custom-call(bf16[1024,4096]{1,0:T(8,128)(2,1)} %queries.3, bf16[1024,4096]{1,0:T(8,128)(2,1)} %grad_out.3, bf16[128,512]{1,0:T(8,128)(2,1)} %keys.1, ...), custom_call_target="tpu_custom_call" | custom-call | tf_op jit(solution)/shard_map/gather/pallas_call | solution.py:712
  38.0 0.0 copy-done.2
  38.0 0.0 copy-done.3
  38.0 0.0 copy-start
  38.0 0.8 copy-done
  38.9 0.0 copy-start.1
  38.9 0.7 copy-done.1
  39.6 36.6 %attend.1 = (bf16[2048,512]{1,0:T(8,128)(2,1)S(1)}, bf16[4,4,4,128,128]{4,3,2,1,0:T(8,128)(2,1)S(1)}, bf16[4,4,4,128,128]{4,3,2,1,0:T(8,128)(2,1)S(1)}, f32[8,128]{1,0:T(8,128)S(1)}) custom-call(s32[16,128]{1,0:T(8,128)S(1)} %copy-done.1, f32[16,8,128]{2,1,0:T(8,128)S(1)} %copy-done, bf16[1024,4096]{1,0:T(8,128)(2,1)} %queries.3, ...), custom_call_target="tpu_custom_call" | custom-call | tf_op jit(solution)/shard_map/attend/pallas_call | solution.py:680
  76.1 47.1 %scatter.1 = (bf16[128,4096]{1,0:T(8,128)(2,1)S(1)}, bf16[128,512]{1,0:T(8,128)(2,1)S(1)}, bf16[128,512]{1,0:T(8,128)(2,1)S(1)}, f32[1,512]{1,0:T(1,128)S(1)}, f32[1,512]{1,0:T(1,128)S(1)}) custom-call(bf16[2048,512]{1,0:T(8,128)(2,1)S(1)} %get-tuple-element.24.dq, bf16[4,4,4,128,128]{4,3,2,1,0:T(8,128)(2,1)S(1)} %get-tuple-element.25.dk, ...), custom_call_target="tpu_custom_call" | custom-call | tf_op jit(solution)/shard_map/scatter/pallas_call | solution.py:748
  123.3 1.0 copy.21
  124.2 0.7 copy.22
  124.9 0.7 copy.23
  125.6 0.6 copy.24
  126.1 0.6 copy.25
Async XLA Ops:
  0.6 37.4 %copy-start.2 = (f32[512]{0:T(512)S(1)}, f32[512]{0:T(512)}, u32[]{:S(2)}) copy-start(f32[512]{0:T(512)} %param.17) | copy-start | bytes 6148
  0.6 37.4 %copy-start.3 = (f32[512]{0:T(512)S(1)}, f32[512]{0:T(512)}, u32[]{:S(2)}) copy-start(f32[512]{0:T(512)} %param.18) | copy-start | bytes 6148
  38.0 0.8 copy-start
  38.9 0.7 copy-start.1
